TPU v7x, 32 devices: a whole 2x2x4 slice. The times are simulated.
32 devices in a mesh: groups: 2 (over y), acq: 8 (over z, x), rng: 2 (over core).
Axes of the slice: x: 2, y: 2, z: 4, core: 2. Of those that a mesh axis runs over, the one named last changes fastest.
Arguments:
- slc: bfloat16 [2, 16, 64, 2048], P(None, ('groups', 'acq'), None, 'rng'), parts along dimension 1, may hold values from -32 to 32, as said below
- map_cell: int32 [16, 256], P('groups', 'rng'), parts along dimension 0, may hold values from 0 to 16383, as said below
Outputs:
- geocoded: float32 [3, 8, 2, 16384], P(None, 'groups', None, ('acq', 'rng')), parts along dimension 1
There are 2 independent parts, one for each index of `groups`. A program takes and returns all parts, laid end to end along the dimension named above; each array names one. Nothing has to cross between parts.
Inputs may be any that keep to these rules, and one draw needn't show every extreme that they name: `slc`: samples of an acquisition share a scene phase with the others, up to a per-sample phase drift. `map_cell`: A map cell is row * 128 + column on a grid of 128 rows; several radar cells may share one, and some map cells receive none. Nothing more is promised about where a radar cell lands.
All inputs are finite; a program needn't handle non-finite values.
Results may differ from a plain program's by a relative error of at most 0.0003.
Values may be sent and summed in bfloat16 or wider, within the bound.
A program may use at most 128 MiB of HBM per device.

v0:
```python
import jax
import jax.numpy as jnp
from jax import lax
from jax.sharding import PartitionSpec as P

LOOK_A = 8
LOOK_R = 8
HALF_W = 4
ROUNDS = 3
MAPC = 16384


def swapped(value, axis, stride):
    mask = 2**stride
    pairs = [(source, source ^ mask) for source in range(lax.axis_size(axis))]
    return lax.ppermute(value, axis, pairs)


def padded_2(shard, sides, width):
    for axis, dim in sides:
        size, length = (lax.axis_size(axis), shard.shape[dim])
        up = [(i, (i + 1) % size) for i in range(size - 1)]
        down = [(j, i) for i, j in up]
        last = lax.slice_in_dim(shard, length - width, length, axis=dim)
        leading = lax.slice_in_dim(shard, 0, width, axis=dim)
        before = lax.ppermute(last, axis, up)
        after = lax.ppermute(leading, axis, down)
        shard = jnp.concatenate([before, shard, after], axis=dim)
    return shard


def look_sum(values_in):
    line_count, col_count = values_in.shape
    return values_in.reshape(line_count // LOOK_A, LOOK_A, col_count // LOOK_R, LOOK_R).sum(
        axis=(1, 3)
    )


def per_device(slc, map_cell):
    acq_count = lax.axis_size("acq")
    rng_count = lax.axis_size("rng")
    acq_rank = lax.axis_index("acq")
    own_block = slc[:, 0]
    line_total = own_block.shape[1]
    half_lines = line_total // 2
    half_looks = half_lines // LOOK_A
    owner_cells = MAPC // acq_count
    piece = owner_cells // rng_count
    map_bins = []
    for round_index in range(ROUNDS):
        upper_flag = acq_rank // 2**round_index % 2
        row_start = upper_flag * half_lines
        mine_rows = lax.dynamic_slice_in_dim(own_block, row_start, half_lines, 1)
        partner_all = swapped(own_block, "acq", round_index)
        their_rows = lax.dynamic_slice_in_dim(partner_all, row_start, half_lines, 1)
        mine_f = mine_rows.astype(jnp.float32)
        their_f = their_rows.astype(jnp.float32)
        sign_flip = (1 - 2 * upper_flag).astype(jnp.float32)
        real_part = mine_f[0] * their_f[0] + mine_f[1] * their_f[1]
        imag_part = (mine_f[1] * their_f[0] - mine_f[0] * their_f[1]) * sign_flip
        power_mine = look_sum(mine_f[0] * mine_f[0] + mine_f[1] * mine_f[1])
        power_their = look_sum(their_f[0] * their_f[0] + their_f[1] * their_f[1])
        inverse = 1.0 / jnp.sqrt(power_mine * power_their + 1e-06)
        gamma = jnp.stack([look_sum(real_part) * inverse, look_sum(imag_part) * inverse])
        padded = padded_2(gamma, (("rng", 2),), HALF_W)
        col_count = gamma.shape[2]
        smooth = jnp.zeros_like(gamma)
        for offset in range(-HALF_W, HALF_W + 1):
            weight = (HALF_W + 1 - abs(offset)) / float((HALF_W + 1) ** 2)
            smooth = smooth + weight * padded[:, :, HALF_W + offset : HALF_W + offset + col_count]
        gain_term = (smooth[0] * smooth[0] + smooth[1] * smooth[1] + 0.01) ** (-0.25)
        filtered = smooth * gain_term[None]
        cell_rows = lax.dynamic_slice_in_dim(
            map_cell, upper_flag * half_looks, half_looks, 0
        ).reshape(-1)
        cell_sums = jnp.zeros((2, MAPC), jnp.float32).at[:, cell_rows].add(filtered.reshape(2, -1))
        map_bins.append(cell_sums)
    stacked = jnp.stack(map_bins)[:, None]
    local_counts = jnp.zeros((MAPC,), jnp.float32).at[map_cell.reshape(-1)].add(1.0)
    shaped = stacked.reshape(ROUNDS, 1, 2, acq_count, rng_count * piece)
    count_rows = local_counts.reshape(1, 1, 1, acq_count, rng_count * piece)
    partial_sum, count_sum = (
        lax.psum_scatter(shaped, "rng", scatter_dimension=4, tiled=True),
        lax.psum_scatter(count_rows, "rng", scatter_dimension=4, tiled=True),
    )
    arrived = lax.all_to_all(partial_sum, "acq", split_axis=3, concat_axis=1, tiled=True)
    reduced = arrived.reshape(ROUNDS, acq_count, 2, piece)
    count_mine = lax.dynamic_slice_in_dim(
        count_sum.reshape(acq_count, piece), acq_rank, 1, 0
    ).reshape(piece)
    divisor = jnp.maximum(count_mine, 1.0)
    results = []
    for round_index in range(ROUNDS):
        stride = 2**round_index
        rows_now = (
            reduced[round_index].reshape(acq_count // (2 * stride), 2, stride, 2, piece).sum(axis=1)
        )
        results.append(rows_now.reshape(acq_count // 2, 2, piece) / divisor)
    return jnp.stack(results)


def solution(mesh):
    in_specs = (P(None, ("groups", "acq"), None, "rng"), P("groups", "rng"))
    out_specs = P(None, "groups", None, ("acq", "rng"))
    return jax.shard_map(
        per_device, mesh=mesh, in_specs=in_specs, out_specs=out_specs, check_vma=False
    )
```

profile of v0, /device:TPU:0, one launch (start us, length us, event | category | flops | bytes accessed | tf_op | source)
XLA Modules:
  0.0 361.2 jit_solution(14497064538894836737)
XLA Ops:
  6.5 2.9 collective-permute-start
  11.1 2.6 collective-permute-start.6
  17.2 2.5 add.339
  33.8 3.0 collective-permute-start.4
  43.8 3.0 collective-permute-start.7
  48.7 6.0 %scatter_custom_fusion = f32[2,16384]{0,1:T(8,128)} fusion(s32[512]{0:T(512)S(1)} %bitcast.191, f32[512,2]{1,0:T(8,128)S(1)} %bitcast.171, f32[]{:T(128)} %constant.75.clone.1), kind=kCustom, calls=%fused_computation.10 | custom fusion | flops 1024 | bytes 131076 | tf_op jit(solution)/shard_map/scatter-add | solution.py:76
  54.6 5.2 %copy.61 = f32[1,1,2,8,2048]{4,2,1,0,3:T(2,128)S(1)} copy(f32[1,1,2,8,2048]{2,4,3,1,0:T(8,128)} %bitcast.162) | data formatting | bytes 262144 | tf_op jit(solution)/shard_map/stack | solution.py:78
  60.2 6.0 %scatter_custom_fusion.1 = f32[2,16384]{0,1:T(8,128)} fusion(s32[512]{0:T(512)S(1)} %bitcast.193, f32[512,2]{1,0:T(8,128)S(1)} %bitcast.172, f32[]{:T(128)} %constant.75.clone.1), kind=kCustom, calls=%fused_computation.8 | custom fusion | flops 1024 | bytes 131076 | tf_op jit(solution)/shard_map/scatter-add | solution.py:76
  66.2 5.2 %copy.62 = f32[1,1,2,8,2048]{4,2,1,0,3:T(2,128)S(1)} copy(f32[1,1,2,8,2048]{2,4,3,1,0:T(8,128)} %bitcast.163) | data formatting | bytes 262144 | tf_op jit(solution)/shard_map/stack | solution.py:78
  71.8 6.0 %scatter_custom_fusion.2 = f32[2,16384]{0,1:T(8,128)} fusion(s32[512]{0:T(512)S(1)} %bitcast.192, f32[512,2]{1,0:T(8,128)S(1)} %bitcast.170, f32[]{:T(128)} %constant.75.clone.1), kind=kCustom, calls=%fused_computation.6 | custom fusion | flops 1024 | bytes 131076 | tf_op jit(solution)/shard_map/scatter-add | solution.py:76
  77.7 5.2 %copy.63 = f32[1,1,2,8,2048]{4,2,1,0,3:T(2,128)S(1)} copy(f32[1,1,2,8,2048]{2,4,3,1,0:T(8,128)} %bitcast.164) | data formatting | bytes 262144 | tf_op jit(solution)/shard_map/stack | solution.py:78
  83.2 43.0 %copy.68 = f32[3,1,2,8,2048]{2,1,0,3,4:T(1,128)} copy(f32[3,1,2,8,2048]{4,2,1,0,3:T(2,128)S(1)} %pad_maximum_fusion.1) | data formatting | bytes 786432
  126.2 91.3 %bitcast_reduce_fusion = f32[2048,8,3,2]{3,2,1,0:T(4,128)} fusion(f32[3,1,2,8,2048]{2,1,0,3,4:T(1,128)} %copy.68), kind=kLoop, calls=%fused_computation.4 | loop fusion | bytes 786432
  217.4 36.2 %reshape.470 = f32[2048,48]{1,0:T(8,128)} reshape(f32[2048,8,3,2]{3,2,1,0:T(4,128)} %bitcast_reduce_fusion) | data formatting | bytes 786432
  253.7 11.0 %reduce-scatter.7.cloned.1.call-done = f32[1024,48]{1,0:T(8,128)} async-done(((f32[2048,48]{1,0:T(8,128)}), f32[1024,48]{1,0:T(8,128)}) %reduce-scatter.7.cloned.1.call-update) | async-done | bytes 196624
  264.7 23.7 %reshape.471 = f32[1024,8,3,1,2]{4,3,2,1,0:T(1,128)} reshape(f32[1024,48]{1,0:T(8,128)} %reduce-scatter.7.cloned.1.call-done) | data formatting | bytes 393216
  288.4 27.8 %copy.69 = f32[3,1,2,8,1024]{4,2,1,0,3:T(2,128)} copy(f32[3,1,2,8,1024]{2,1,0,3,4:T(1,128)} %bitcast.161) | data formatting | bytes 393216
  316.2 5.8 %all-to-all-start = ((f32[3,1,2,8,1024]{4,2,1,0,3:T(2,128)}), f32[3,1,2,8,1024]{4,2,1,0,3:T(2,128)S(1)}, u32[]{:S(2)}, u32[]{:S(2)}) async-start(f32[3,1,2,8,1024]{4,2,1,0,3:T(2,128)} %copy.69), calls=%async_computation | async-start | bytes 393216 | tf_op jit(solution)/shard_map/all_to_all | solution.py:86
  322.0 6.0 %scatter_custom_fusion.3 = f32[16384]{0:T(1024)S(1)} fusion(s32[1024]{0:T(1024)S(1)} %bitcast.190, f32[1024]{0:T(1024)S(1)} %broadcast.205, f32[]{:T(128)} %constant.75.clone.1), kind=kCustom, calls=%fused_computation.40 | custom fusion | flops 1024 | bytes 65540 | tf_op jit(solution)/shard_map/scatter-add | solution.py:79
  328.7 8.9 %reduce-scatter.5.cloned.1.call-done = f32[1,1,1,8,1024]{4,3,2,1,0:T(8,128)} async-done(((f32[1,1,1,8,2048]{4,3,2,1,0:T(8,128)}), f32[1,1,1,8,1024]{4,3,2,1,0:T(8,128)}) %reduce-scatter.5.cloned.1.call-update) | async-done | bytes 32784 | tf_op jit(solution)/shard_map/reduce_scatter | solution.py:84
  339.2 2.0 copy.73
  343.2 2.9 bitcast_divide_fusion.2
  346.1 3.2 pad_maximum_fusion
  349.3 5.1 %copy.67 = f32[3,4,2,1024]{3,2,1,0:T(2,128)} copy(f32[3,4,2,1024]{2,3,1,0:T(8,128)} %pad_maximum_fusion) | data formatting | bytes 196608 | tf_op jit(solution)/shard_map/stack | solution.py:99
  (89 shorter events, 32.9 us)
Async XLA Ops:
  6.5 258.1 %reduce-scatter.7.cloned.1.call-start = ((), (), s32[]{:S(2)}) async-start(), calls=%async_computation.4 | async-start | bytes 1572864
  6.5 9.5 %collective-permute-start = (bf16[2,64,1024]{2,1,0:T(8,128)(2,1)}, bf16[2,64,1024]{2,1,0:T(8,128)(2,1)S(1)}, u32[]{:S(2)}, u32[]{:S(2)}) collective-permute-start(bf16[2,64,1024]{2,1,0:T(8,128)(2,1)} %bitcast.167), channel_id=1, source_target_pairs={{0,2},{2,0},{4,6},{6,4},{8,10},{10,8},{12,14},{14,12},{1,3},{3,1},... | collective-permute-start | bytes 786440 | tf_op jit(solution)/shard_map/ppermute | solution.py:16
  9.5 17.7 %collective-permute-start.3 = (bf16[2,64,1024]{2,1,0:T(8,128)(2,1)}, bf16[2,64,1024]{2,1,0:T(8,128)(2,1)}, u32[]{:S(2)}, u32[]{:S(2)}) collective-permute-start(bf16[2,64,1024]{2,1,0:T(8,128)(2,1)} %bitcast.168), channel_id=1, source_target_pairs={{0,4},{2,6},{4,0},{6,2},{8,12},{10,14},{12,8},{14,10},{1,5},{3,7},... | collective-permute-start | bytes 786440 | tf_op jit(solution)/shard_map/ppermute | solution.py:16
  11.1 27.0 %collective-permute-start.6 = (bf16[2,64,1024]{2,1,0:T(8,128)(2,1)}, bf16[2,64,1024]{2,1,0:T(8,128)(2,1)S(1)}, u32[]{:S(2)}, u32[]{:S(2)}) collective-permute-start(bf16[2,64,1024]{2,1,0:T(8,128)(2,1)} %bitcast.169), channel_id=1, source_target_pairs={{0,8},{2,10},{4,12},{6,14},{8,0},{10,2},{12,4},{14,6},{1,9},{3,11}... | collective-permute-start | bytes 786440 | tf_op jit(solution)/shard_map/ppermute | solution.py:16
  24.6 22.2 %collective-permute-start.1 = (f32[2,4,4]{2,1,0:T(4,128)S(1)}, f32[2,4,4]{2,1,0:T(4,128)S(1)}, u32[]{:S(2)}, u32[]{:S(2)}) collective-permute-start(f32[2,4,4]{2,1,0:T(4,128)S(1)} %get-tuple-element.28), channel_id=1, source_target_pairs={{0,1},{2,3},{4,5},{6,7},{8,9},{10,11},{12,13},{14,15},{16,17},{18,... | collective-permute-start | bytes 392 | tf_op jit(solution)/shard_map/ppermute | solution.py:26
  25.9 22.4 %collective-permute-start.2 = (f32[2,4,4]{2,1,0:T(4,128)S(1)}, f32[2,4,4]{2,1,0:T(4,128)S(1)}, u32[]{:S(2)}, u32[]{:S(2)}) collective-permute-start(f32[2,4,4]{2,1,0:T(4,128)S(1)} %get-tuple-element.29), channel_id=1, source_target_pairs={{1,0},{3,2},{5,4},{7,6},{9,8},{11,10},{13,12},{15,14},{17,16},{19,... | collective-permute-start | bytes 392 | tf_op jit(solution)/shard_map/ppermute | solution.py:27
  33.8 26.1 %collective-permute-start.4 = (f32[2,4,4]{2,1,0:T(4,128)S(1)}, f32[2,4,4]{2,1,0:T(4,128)S(1)}, u32[]{:S(2)}, u32[]{:S(2)}) collective-permute-start(f32[2,4,4]{2,1,0:T(4,128)S(1)} %get-tuple-element.37), channel_id=1, source_target_pairs={{0,1},{2,3},{4,5},{6,7},{8,9},{10,11},{12,13},{14,15},{16,17},{18,... | collective-permute-start | bytes 392 | tf_op jit(solution)/shard_map/ppermute | solution.py:26
  36.8 23.1 %collective-permute-start.5 = (f32[2,4,4]{2,1,0:T(4,128)S(1)}, f32[2,4,4]{2,1,0:T(4,128)S(1)}, u32[]{:S(2)}, u32[]{:S(2)}) collective-permute-start(f32[2,4,4]{2,1,0:T(4,128)S(1)} %get-tuple-element.38), channel_id=1, source_target_pairs={{1,0},{3,2},{5,4},{7,6},{9,8},{11,10},{13,12},{15,14},{17,16},{19,... | collective-permute-start | bytes 392 | tf_op jit(solution)/shard_map/ppermute | solution.py:27
  43.8 27.6 %collective-permute-start.7 = (f32[2,4,4]{2,1,0:T(4,128)S(1)}, f32[2,4,4]{2,1,0:T(4,128)S(1)}, u32[]{:S(2)}, u32[]{:S(2)}) collective-permute-start(f32[2,4,4]{2,1,0:T(4,128)S(1)} %get-tuple-element.43), channel_id=1, source_target_pairs={{0,1},{2,3},{4,5},{6,7},{8,9},{10,11},{12,13},{14,15},{16,17},{18,... | collective-permute-start | bytes 392 | tf_op jit(solution)/shard_map/ppermute | solution.py:26
  46.8 24.6 %collective-permute-start.8 = (f32[2,4,4]{2,1,0:T(4,128)S(1)}, f32[2,4,4]{2,1,0:T(4,128)S(1)}, u32[]{:S(2)}, u32[]{:S(2)}) collective-permute-start(f32[2,4,4]{2,1,0:T(4,128)S(1)} %get-tuple-element.44), channel_id=1, source_target_pairs={{1,0},{3,2},{5,4},{7,6},{9,8},{11,10},{13,12},{15,14},{17,16},{19,... | collective-permute-start | bytes 392 | tf_op jit(solution)/shard_map/ppermute | solution.py:27
  288.4 33.6 %copy-start = (s32[8,128]{1,0:T(8,128)S(1)}, s32[8,128]{1,0:T(8,128)}, u32[]{:S(2)}) copy-start(s32[8,128]{1,0:T(8,128)} %param.3) | copy-start | bytes 12292
  316.2 22.2 %all-to-all-start = ((f32[3,1,2,8,1024]{4,2,1,0,3:T(2,128)}), f32[3,1,2,8,1024]{4,2,1,0,3:T(2,128)S(1)}, u32[]{:S(2)}, u32[]{:S(2)}) async-start(f32[3,1,2,8,1024]{4,2,1,0,3:T(2,128)} %copy.69), calls=%async_computation | async-start | bytes 393216 | tf_op jit(solution)/shard_map/all_to_all | solution.py:86
  322.0 15.7 %reduce-scatter.5.cloned.1.call-start = ((), (), s32[]{:S(2)}) async-start(), calls=%async_computation.3 | async-start | bytes 98304 | tf_op jit(solution)/shard_map/reduce_scatter | solution.py:84
Sparse Core Ops, SparseCore 0:
  253.8 10.8 reduce-scatter.6
  328.8 8.7 reduce-scatter.4
where the time goes:
time: 363 us; the launch traced here: 361 us
  local copies, waits for them, and re-layouts  264 us (73%)
  other arithmetic  38.4 us (11%)
  starting transfers between devices  24.3 us (7%)
  waiting for transfers between devices  20.3 us (6%)
  between operations  13.9 us (4%)
    unnamed x13, local copies, waits for them, and re-layouts  227 us
    scatter-add x3, other arithmetic, per_device(): jnp.zeros((2, MAPC), jnp.float32).at[:, cell_rows]  17.9 us
    another operation x3, local copies, waits for them, and re-layouts, per_device(): stacked = jnp.stack(map_bins)[:, None]  15.6 us
    unnamed x3, waiting for transfers between devices  11 us
    reduce_scatter x1, waiting for transfers between devices, per_device(): lax.psum_scatter(count_rows, 'rng', scatter_dimension=4, tiled=True)  8.93 us
    ppermute x3, starting transfers between devices, padded_2(): before = lax.ppermute(last, axis, up)  7.34 us
  transfers between devices with their start and end apart: 12, of which 3 were waited for; matrix products, arithmetic and copies ran while one was open for 15% of the time, Pallas kernels for 0%

commit v1 on v0

v1 whole, which is shorter than its diff:
```python
import functools

import jax
import jax.numpy as jnp
from jax import lax
from jax.experimental import pallas as pl
from jax.experimental.pallas import tpu as pltpu
from jax.sharding import PartitionSpec as P

LOOK_A = 8
LOOK_R = 8
HALF_W = 4
ROUNDS = 3
MAPC = 16384
BLOCK = 2**ROUNDS
PAIRS = BLOCK // 2
ROWS = ROUNDS * PAIRS * 2
MESH = pl.DeviceIdType.MESH
F32 = jnp.float32
BF16 = jnp.bfloat16


def split3(value):
    first = value.astype(BF16).astype(F32)
    rest = value - first
    second = rest.astype(BF16).astype(F32)
    return first, second, rest - second


def iota(shape, dim):
    return lax.broadcasted_iota(jnp.int32, shape, dim)


def kernel(
    acq_count,
    rng_count,
    slc_ref,
    map_ref,
    out_ref,
    samples,
    cells,
    gathered,
    one_hot,
    looks,
    band,
    own_sem,
    send_sem,
    recv_sem,
    map_send,
    map_recv,
    gather_send,
    gather_recv,
):
    group = acq_count * rng_count
    blocks = acq_count // BLOCK
    acq_rank = lax.axis_index("acq")
    rng_rank = lax.axis_index("rng")
    flat = acq_rank * rng_count + rng_rank
    base = acq_rank // BLOCK * BLOCK
    member = acq_rank % BLOCK
    tile_lines, tile_cols = samples.shape[2:]
    halves = slc_ref.shape[3] // tile_cols
    piece = out_ref.shape[2]

    def peer(step):
        other = (flat + step) % group
        return {"acq": other // rng_count, "rng": other % rng_count}, other

    def greet(step, carry):
        pl.semaphore_signal(barrier, inc=1, device_id=peer(step)[0], device_id_type=MESH)
        return carry

    barrier = pltpu.get_barrier_semaphore()
    lax.fori_loop(1, group, greet, 0)
    pl.semaphore_wait(barrier, group - 1)

    def tile_of(target):
        line = pl.multiple_of(target // halves * tile_lines, tile_lines)
        col = pl.multiple_of(target % halves * tile_cols, tile_cols)
        return slc_ref.at[:, 0, pl.ds(line, tile_lines), pl.ds(col, tile_cols)]

    sends = []
    for step in (4, 3, 5, 2, 6, 1, 7):
        target = (member + step) % BLOCK
        copy = pltpu.make_async_remote_copy(
            src_ref=tile_of(target),
            dst_ref=samples.at[member],
            send_sem=send_sem.at[step],
            recv_sem=recv_sem.at[member],
            device_id={"acq": base + target},
            device_id_type=MESH,
        )
        copy.start()
        sends.append(copy)
    own = pltpu.make_async_copy(tile_of(member), samples.at[member], own_sem)
    own.start()
    map_copy = pltpu.make_async_remote_copy(
        src_ref=map_ref,
        dst_ref=cells.at[rng_rank],
        send_sem=map_send,
        recv_sem=map_recv,
        device_id={"rng": 1 - rng_rank},
        device_id_type=MESH,
    )
    map_copy.start()
    cells[rng_rank] = map_ref[...]

    look_cells = tile_cols // LOOK_R
    lanes = looks.shape[1]
    looks[...] = jnp.where(
        iota(looks.shape, 0) // LOOK_R == iota(looks.shape, 1) % look_cells, 1.0, 0.0
    ).astype(BF16)
    source = iota(band.shape, 0)
    target = iota(band.shape, 1)
    wide = rng_count * halves * look_cells
    source_cell = source // lanes * look_cells + source % look_cells
    source_look = source % lanes // look_cells
    gap = jnp.abs(source_cell - target % wide)
    weight = jnp.where(source_look == target // wide, jnp.maximum(HALF_W + 1 - gap, 0), 0)
    band[...] = weight.astype(F32).astype(BF16)

    map_copy.wait()
    place = iota((piece, lanes), 0) + flat * piece
    for line in range(map_ref.shape[0]):
        for core in range(rng_count):
            row = cells[core, line : line + 1, :]
            one_hot[:, pl.ds((line * rng_count + core) * lanes, lanes)] = jnp.where(
                place == row, 1.0, 0.0
            ).astype(BF16)

    own.wait()
    for step in (1, 7, 2, 6, 3, 5, 4):
        origin = (member + step) % BLOCK
        pltpu.make_async_remote_copy(
            src_ref=samples.at[origin],
            dst_ref=samples.at[origin],
            send_sem=send_sem.at[step],
            recv_sem=recv_sem.at[origin],
            device_id={"acq": base + origin},
            device_id_type=MESH,
        ).wait_recv()

    real = [samples[a, 0].astype(F32) for a in range(BLOCK)]
    imag = [samples[a, 1].astype(F32) for a in range(BLOCK)]
    products = []
    pairs = []
    for r in range(ROUNDS):
        stride = 2**r
        for k in range(PAIRS):
            low = k // stride * 2 * stride + k % stride
            up = low + stride
            pairs.append((low, up))
            products.append(real[low] * real[up] + imag[low] * imag[up])
            products.append(imag[low] * real[up] - real[low] * imag[up])
    for a in range(BLOCK):
        products.append(real[a] * real[a] + imag[a] * imag[a])
    stacked = jnp.concatenate(products, axis=0)
    weights = looks[...]
    summed = sum(
        jnp.dot(part.astype(BF16), weights, preferred_element_type=F32)
        for part in reversed(split3(stacked))
    )
    summed = summed.reshape(len(products), tile_lines, lanes)
    lane = iota((1, 1, lanes), 2)
    chosen = jnp.where(lane < look_cells, summed[:, :LOOK_A], summed[:, LOOK_A:])
    sums = jnp.sum(chosen, axis=1)
    power = sums[ROWS:]
    power_low = jnp.concatenate([power[low : low + 1] for low, _ in pairs for _ in range(2)], axis=0)
    power_up = jnp.concatenate([power[up : up + 1] for _, up in pairs for _ in range(2)], axis=0)
    inverse = 1.0 / jnp.sqrt(power_low * power_up + 1e-06)
    gathered[flat] = sums[:ROWS] * inverse

    def gather_copy(step, index, slot):
        return pltpu.make_async_remote_copy(
            src_ref=gathered.at[slot],
            dst_ref=gathered.at[slot],
            send_sem=gather_send.at[step],
            recv_sem=gather_recv.at[slot],
            device_id=index,
            device_id_type=MESH,
        )

    def gather_start(step, carry):
        gather_copy(step, peer(step)[0], flat).start()
        return carry

    def gather_wait(step, carry):
        index, other = peer(step)
        gather_copy(step, index, other).wait_recv()
        return carry

    lax.fori_loop(1, group, gather_start, 0)
    for copy in sends:
        copy.wait_send()
    map_weights = one_hot[...]
    band_weights = band[...]
    lax.fori_loop(1, group, gather_wait, 0)

    quarters = BLOCK // halves
    even = iota((quarters * ROWS, 1), 0) % 2 == 0
    ones = jnp.ones((8, quarters * band.shape[1]), F32)

    def finish(block, carry):
        rows = []
        for q in range(quarters):
            parts = [
                gathered[(block * BLOCK + q * halves + h) * rng_count + c]
                for c in range(rng_count)
                for h in range(halves)
            ]
            rows.append(jnp.concatenate(parts, axis=1))
        gamma = jnp.concatenate(rows, axis=0)
        smooth = sum(
            jnp.dot(part.astype(BF16), band_weights, preferred_element_type=F32)
            for part in reversed(split3(gamma))
        ) * (1.0 / (HALF_W + 1) ** 2)
        square = smooth * smooth
        count = square.shape[0]
        partner = jnp.where(even, pltpu.roll(square, count - 1, 0), pltpu.roll(square, 1, 0))
        filtered = smooth * lax.rsqrt(jnp.sqrt(square + partner + 0.01))
        flat_rows = jnp.concatenate(
            [filtered[q * ROWS : (q + 1) * ROWS] for q in range(quarters)], axis=1
        )
        left = jnp.concatenate([*split3(flat_rows), ones], axis=0).astype(BF16)
        total = lax.dot_general(
            left, map_weights, (((1,), (1,)), ((), ())), preferred_element_type=F32
        )
        divisor = jnp.maximum(total[3 * ROWS : 3 * ROWS + 1], 1.0)
        result = (total[2 * ROWS : 3 * ROWS] + total[ROWS : 2 * ROWS] + total[:ROWS]) / divisor
        for r in range(ROUNDS):
            span = 2 * PAIRS
            start = pl.multiple_of(block * span, span)
            out_ref[r, pl.ds(start, span), :] = result[r * span : (r + 1) * span]
        return carry

    lax.fori_loop(0, blocks, finish, 0)

    def gather_sent(step, carry):
        gather_copy(step, peer(step)[0], flat).wait_send()
        return carry

    lax.fori_loop(1, group, gather_sent, 0)


def per_device(slc, map_cell):
    acq_count = lax.axis_size("acq")
    rng_count = lax.axis_size("rng")
    group = acq_count * rng_count
    lines, cols = slc.shape[2:]
    tile_lines = 2 * LOOK_A
    halves = BLOCK * tile_lines // lines
    tile_cols = cols // halves
    lanes = 2 * tile_cols // LOOK_R
    wide = 2 * rng_count * cols // LOOK_R
    radar = map_cell.shape[0] * map_cell.shape[1] * rng_count
    piece = MAPC // group
    pairs = acq_count // 2
    dma = pltpu.SemaphoreType.DMA
    result = pl.pallas_call(
        functools.partial(kernel, acq_count, rng_count),
        out_shape=jax.ShapeDtypeStruct((ROUNDS, pairs * 2, piece), F32),
        in_specs=[
            pl.BlockSpec(memory_space=pl.ANY),
            pl.BlockSpec(memory_space=pltpu.VMEM),
        ],
        out_specs=pl.BlockSpec(memory_space=pltpu.VMEM),
        scratch_shapes=[
            pltpu.VMEM((BLOCK, 2, tile_lines, tile_cols), BF16),
            pltpu.VMEM((rng_count,) + map_cell.shape, jnp.int32),
            pltpu.VMEM((group, ROWS, lanes), F32),
            pltpu.VMEM((piece, radar), BF16),
            pltpu.VMEM((tile_cols, lanes), BF16),
            pltpu.VMEM((wide, wide), BF16),
            dma,
            dma((BLOCK,)),
            dma((BLOCK,)),
            dma,
            dma,
            dma((group,)),
            dma((group,)),
        ],
        compiler_params=pltpu.CompilerParams(
            collective_id=0, has_side_effects=True, vmem_limit_bytes=40 * 2**20
        ),
    )(slc, map_cell)
    return result.reshape(ROUNDS, pairs, 2, piece)


def solution(mesh):
    in_specs = (P(None, ("groups", "acq"), None, "rng"), P("groups", "rng"))
    out_specs = P(None, "groups", None, ("acq", "rng"))
    return jax.shard_map(
        per_device, mesh=mesh, in_specs=in_specs, out_specs=out_specs, check_vma=False
    )
```

time: 363 us -> 23.7 us (0.07)
  local copies, waits for them, and re-layouts: 264 us -> 2.33 us
  other arithmetic: 38.4 us -> 0 us
  starting transfers between devices: 24.3 us -> 0 us
  Pallas kernels: 0 us -> 21.1 us
  waiting for transfers between devices: 20.3 us -> 0 us
  between operations: 13.9 us -> 0.01 us
    unnamed x13 -> x4, local copies, waits for them, and re-layouts: 227 us -> 1.64 us
    scatter-add x4 -> x0, other arithmetic: 23.9 us -> none  [the longest x3 17.9 us: per_device(): jnp.zeros((2, MAPC), jnp.float32).at[:, cell_rows]]
    pallas_call x0 -> x1, Pallas kernels: none -> 21.1 us  [per_device(): pl.pallas_call(functools.partial(kernel, acq_count, rng_count), out_shape...]
    another operation x5 -> x0, local copies, waits for them, and re-layouts: 20.7 us -> none  [the longest x3 15.6 us: per_device(): stacked = jnp.stack(map_bins)[:, None]]
    ppermute x9 -> x0, starting transfers between devices: 18.5 us -> none  [the longest x3 7.34 us: padded_2(): before = lax.ppermute(last, axis, up)]
    add x9 -> x0, local copies, waits for them, and re-layouts: 11.6 us -> none  [the longest x3 4.8 us: per_device(): power_mine = look_sum(mine_f[0] * mine_f[0] + mine_f[1] * mine_f[1])]
    unnamed x3 -> x0, waiting for transfers between devices: 11 us -> none
    reduce_scatter x1 -> x0, waiting for transfers between devices: 8.93 us -> none  [per_device(): lax.psum_scatter(count_rows, 'rng', scatter_dimension=4, tiled=True)]
  transfers between devices with their start and end apart: 12 -> 0, of which waited for: 3 -> 0; matrix products, arithmetic and copies ran while one was open for 15% -> 0% of each run, Pallas kernels for 0% -> 0%
where the time goes in v1:
time: 23.7 us; the launch traced here: 23.5 us
  Pallas kernels  21.1 us (89%)
  local copies, waits for them, and re-layouts  2.33 us (10%)
    pallas_call x1, Pallas kernels, per_device(): pl.pallas_call(functools.partial(kernel, acq_count, rng_count), out_shape...  21.1 us
    unnamed x4, local copies, waits for them, and re-layouts  1.64 us
    reshape x1, local copies, waits for them, and re-layouts, per_device(): return result.reshape(ROUNDS, pairs, 2, piece)  0.7 us

profile of v1, /device:TPU:0, one launch (start us, length us, event | category | flops | bytes accessed | tf_op | source)
XLA Modules:
  0.0 23.5 jit_solution(17749629564459178166)
XLA Ops:
  0.0 0.0 copy-start
  0.0 0.9 %copy-done = bf16[2,1,64,1024]{3,2,1,0:T(8,128)(2,1)S(1)} copy-done((bf16[2,1,64,1024]{3,2,1,0:T(8,128)(2,1)S(1)}, bf16[2,1,64,1024]{3,2,1,0:T(8,128)(2,1)}, u32[]{:S(2)}) %copy-start) | copy-done | bytes 262168
  1.0 0.0 copy-start.1
  1.0 0.7 %copy-done.1 = s32[8,128]{1,0:T(8,128)S(1)} copy-done((s32[8,128]{1,0:T(8,128)S(1)}, s32[8,128]{1,0:T(8,128)}, u32[]{:S(2)}) %copy-start.1) | copy-done | bytes 4120
  1.6 21.1 %shard_map.28 = f32[3,8,1024]{2,1,0:T(8,128)S(1)} custom-call(bf16[2,1,64,1024]{3,2,1,0:T(8,128)(2,1)S(1)} %copy-done, s32[8,128]{1,0:T(8,128)S(1)} %copy-done.1), custom_call_target="tpu_custom_call" | custom-call | tf_op jit(solution)/shard_map/pallas_call | solution.py:259
  22.8 0.7 %reshape.3 = f32[3,4,2,1024]{3,2,1,0:T(2,128)} reshape(f32[3,8,1024]{2,1,0:T(8,128)S(1)} %shard_map.28) | data formatting | bytes 196608 | tf_op jit(solution)/shard_map/reshape | solution.py:286
Async XLA Ops:
  0.0 0.9 %copy-start = (bf16[2,1,64,1024]{3,2,1,0:T(8,128)(2,1)S(1)}, bf16[2,1,64,1024]{3,2,1,0:T(8,128)(2,1)}, u32[]{:S(2)}) copy-start(bf16[2,1,64,1024]{3,2,1,0:T(8,128)(2,1)} %slc_ref.1) | copy-start | bytes 786436
  1.0 0.7 %copy-start.1 = (s32[8,128]{1,0:T(8,128)S(1)}, s32[8,128]{1,0:T(8,128)}, u32[]{:S(2)}) copy-start(s32[8,128]{1,0:T(8,128)} %map_ref.1) | copy-start | bytes 12292

commit v2 on v1

v2 whole, which is shorter than its diff:
```python
import functools

import jax
import jax.numpy as jnp
from jax import lax
from jax.experimental import pallas as pl
from jax.experimental.pallas import tpu as pltpu
from jax.sharding import PartitionSpec as P

LOOK_A = 8
LOOK_R = 8
HALF_W = 4
ROUNDS = 3
MAPC = 16384
BLOCK = 2**ROUNDS
PAIRS = BLOCK // 2
SPAN = 2 * PAIRS
ROWS = ROUNDS * SPAN
HALF_PAIRS = ((0, 1), (2, 3), (0, 2), (1, 3))
MESH = pl.DeviceIdType.MESH
F32 = jnp.float32
BF16 = jnp.bfloat16


def split(value, terms):
    parts = []
    for _ in range(terms - 1):
        parts.append(value.astype(BF16).astype(F32))
        value = value - parts[-1]
    return [*parts, value]


def pair_products(low, up):
    real = low[0] * up[0] + low[1] * up[1]
    imag = low[1] * up[0] - low[0] * up[1]
    return [real, imag]


def power_product(sample):
    return [sample[0] * sample[0] + sample[1] * sample[1]]


def iota(shape, dim):
    return lax.broadcasted_iota(jnp.int32, shape, dim)


def kernel(
    acq_count,
    rng_count,
    slc_ref,
    map_ref,
    out_ref,
    samples,
    cells,
    gathered,
    one_hot,
    looks,
    band,
    own_sem,
    send_sem,
    recv_sem,
    map_send,
    map_recv,
    gather_send,
    gather_recv,
):
    group = acq_count * rng_count
    blocks = acq_count // BLOCK
    acq_rank = lax.axis_index("acq")
    rng_rank = lax.axis_index("rng")
    flat = acq_rank * rng_count + rng_rank
    base = acq_rank // BLOCK * BLOCK
    member = acq_rank % BLOCK
    tile_lines, tile_cols = samples.shape[2:]
    halves = slc_ref.shape[3] // tile_cols
    piece = out_ref.shape[2]

    def peer(far, core):
        other = acq_rank + far
        other = jnp.where(other >= acq_count, other - acq_count, other)
        side = rng_rank + core
        side = jnp.where(side >= rng_count, side - rng_count, side)
        return {"acq": other, "rng": side}, other * rng_count + side

    def for_peers(body):
        for core in range(1, rng_count):
            body(0, core)
        if acq_count <= 2 * BLOCK:
            for far in range(1, acq_count):
                for core in range(rng_count):
                    body(far, core)
            return

        def distant(far, carry):
            for core in range(rng_count):
                body(far, core)
            return carry

        lax.fori_loop(1, acq_count, distant, 0)

    barrier = pltpu.get_barrier_semaphore()

    def greet(far, core):
        pl.semaphore_signal(barrier, inc=1, device_id=peer(far, core)[0], device_id_type=MESH)

    for_peers(greet)
    pl.semaphore_wait(barrier, group - 1)

    def tile_of(target):
        line = pl.multiple_of(target // halves * tile_lines, tile_lines)
        col = pl.multiple_of(target % halves * tile_cols, tile_cols)
        return slc_ref.at[:, 0, pl.ds(line, tile_lines), pl.ds(col, tile_cols)]

    near = member // PAIRS * PAIRS
    distant = PAIRS - near
    sends = []
    for step in (4, 5, 6, 7, 1, 2, 3):
        target = (near if step < PAIRS else distant) + (member + step) % PAIRS
        copy = pltpu.make_async_remote_copy(
            src_ref=tile_of(target),
            dst_ref=samples.at[member],
            send_sem=send_sem.at[step],
            recv_sem=recv_sem.at[member],
            device_id={"acq": base + target},
            device_id_type=MESH,
        )
        copy.start()
        sends.append(copy)
    own = pltpu.make_async_copy(tile_of(member), samples.at[member], own_sem)
    own.start()
    map_copy = pltpu.make_async_remote_copy(
        src_ref=map_ref,
        dst_ref=cells.at[rng_rank],
        send_sem=map_send,
        recv_sem=map_recv,
        device_id={"rng": 1 - rng_rank},
        device_id_type=MESH,
    )
    map_copy.start()
    cells[rng_rank] = map_ref[...]

    look_cells = tile_cols // LOOK_R
    lanes = looks.shape[1]
    looks[...] = jnp.where(
        iota(looks.shape, 0) // LOOK_R == iota(looks.shape, 1) % look_cells, 1.0, 0.0
    ).astype(BF16)
    source = iota(band.shape, 0)
    target = iota(band.shape, 1)
    wide = rng_count * halves * look_cells
    source_cell = source // lanes * look_cells + source % look_cells
    source_look = source % lanes // look_cells
    gap = jnp.abs(source_cell - target % wide)
    weight = jnp.where(source_look == target // wide, jnp.maximum(HALF_W + 1 - gap, 0), 0)
    band[...] = weight.astype(F32).astype(BF16)

    map_copy.wait()
    columns = cells[...].reshape(rng_count * map_ref.shape[0], lanes).astype(F32).T
    place = iota((lanes, piece), 1).astype(F32) + (flat * piece).astype(F32)
    for line in range(map_ref.shape[0]):
        for core in range(rng_count):
            row = core * map_ref.shape[0] + line
            one_hot[pl.ds((line * rng_count + core) * lanes, lanes), :] = jnp.where(
                place == columns[:, row : row + 1], 1.0, 0.0
            ).astype(BF16)

    own.wait()
    look_weights = looks[...]
    lane = iota((1, 1, lanes), 2)

    def sample_arrival(origin):
        return pltpu.make_async_remote_copy(
            src_ref=samples.at[origin],
            dst_ref=samples.at[origin],
            send_sem=send_sem.at[0],
            recv_sem=recv_sem.at[origin],
            device_id={"acq": base + origin},
            device_id_type=MESH,
        )

    def load(origin):
        return samples[origin, 0].astype(F32), samples[origin, 1].astype(F32)

    def look_sums(products):
        stacked = jnp.concatenate(products, axis=0)
        summed = sum(
            jnp.dot(part.astype(BF16), look_weights, preferred_element_type=F32)
            for part in reversed(split(stacked, 3))
        )
        summed = summed.reshape(len(products), tile_lines, lanes)
        chosen = jnp.where(lane < look_cells, summed[:, :LOOK_A], summed[:, LOOK_A:])
        return jnp.sum(chosen, axis=1)

    def coherence(sums, power_low, power_up):
        low = jnp.concatenate([p for p in power_low for _ in range(2)], axis=0)
        up = jnp.concatenate([p for p in power_up for _ in range(2)], axis=0)
        return sums * (1.0 / jnp.sqrt(low * up + 1e-06))

    def half_products(four):
        products = []
        for low, up in HALF_PAIRS:
            products += pair_products(four[low], four[up])
        for sample in four:
            products += power_product(sample)
        return products

    def half_coherence(sums):
        power = [sums[SPAN + a : SPAN + a + 1] for a in range(PAIRS)]
        gamma = coherence(
            sums[:SPAN], [power[low] for low, _ in HALF_PAIRS], [power[up] for _, up in HALF_PAIRS]
        )
        return gamma, power

    def gather_copy(far, core, late, arriving):
        index, other = peer(far, core)
        slot = other if arriving else flat
        rows = pl.ds(SPAN, ROWS - SPAN) if late else pl.ds(0, SPAN)
        return pltpu.make_async_remote_copy(
            src_ref=gathered.at[slot, rows],
            dst_ref=gathered.at[slot, rows],
            send_sem=gather_send.at[late, far * rng_count + core],
            recv_sem=gather_recv.at[late, slot],
            device_id=index,
            device_id_type=MESH,
        )

    for step in range(1, PAIRS):
        sample_arrival(near + (member + step) % PAIRS).wait_recv()
    near_sums = look_sums(half_products([load(near + a) for a in range(PAIRS)]))
    gathered[flat, :SPAN], near_power = half_coherence(near_sums)
    for_peers(lambda far, core: gather_copy(far, core, 0, False).start())

    for step in range(PAIRS):
        sample_arrival(distant + (member + step) % PAIRS).wait_recv()
    products = half_products([load(distant + a) for a in range(PAIRS)])
    for a in range(PAIRS):
        products += pair_products(load(a), load(PAIRS + a))
    late_sums = look_sums(products)
    half_rows = SPAN + PAIRS
    far_gamma, far_power = half_coherence(late_sums[:half_rows])
    gathered[flat, SPAN:] = jnp.concatenate(
        [far_gamma, coherence(late_sums[half_rows:], near_power, far_power)], axis=0
    )
    for_peers(lambda far, core: gather_copy(far, core, 1, False).start())
    for copy in sends:
        copy.wait_send()
    for late in range(2):
        for_peers(lambda far, core: gather_copy(far, core, late, True).wait_recv())

    quarters = BLOCK // halves
    even = iota((quarters * ROWS, 1), 0) % 2 == 0
    ones = jnp.ones((8, quarters * band.shape[1]), F32)

    def piece_of(block, i, c):
        slot = (block * BLOCK + i) * rng_count + c
        if i < PAIRS:
            return gathered[slot]
        return jnp.concatenate(
            [gathered[slot, SPAN : 2 * SPAN], gathered[slot, :SPAN], gathered[slot, 2 * SPAN :]],
            axis=0,
        )

    def finish(block, carry):
        rows = []
        for q in range(quarters):
            parts = [
                piece_of(block, q * halves + h, c)
                for c in range(rng_count)
                for h in range(halves)
            ]
            rows.append(jnp.concatenate(parts, axis=1))
        gamma = jnp.concatenate(rows, axis=0)
        smooth = sum(
            jnp.dot(part.astype(BF16), band[...], preferred_element_type=F32)
            for part in reversed(split(gamma, 2))
        ) * (1.0 / (HALF_W + 1) ** 2)
        square = smooth * smooth
        count = square.shape[0]
        partner = jnp.where(even, pltpu.roll(square, count - 1, 0), pltpu.roll(square, 1, 0))
        filtered = smooth * lax.rsqrt(jnp.sqrt(square + partner + 0.01))
        flat_rows = jnp.concatenate(
            [filtered[q * ROWS : (q + 1) * ROWS] for q in range(quarters)], axis=1
        )
        left = jnp.concatenate([*split(flat_rows, 2), ones], axis=0).astype(BF16)
        total = jnp.dot(left, one_hot[...], preferred_element_type=F32)
        divisor = jnp.maximum(total[2 * ROWS : 2 * ROWS + 1], 1.0)
        result = (total[ROWS : 2 * ROWS] + total[:ROWS]) / divisor
        start = pl.multiple_of(block * SPAN, SPAN)
        low, high, cross = result[:SPAN], result[SPAN : 2 * SPAN], result[2 * SPAN :]
        for r in range(2):
            rows = slice(r * PAIRS, (r + 1) * PAIRS)
            both = jnp.concatenate([low[rows], high[rows]], axis=0)
            out_ref[r, pl.ds(start, SPAN), :] = both
        out_ref[2, pl.ds(start, SPAN), :] = cross
        return carry

    lax.fori_loop(0, blocks, finish, 0)

    for late in range(2):
        for_peers(lambda far, core: gather_copy(far, core, late, False).wait_send())


def per_device(slc, map_cell):
    acq_count = lax.axis_size("acq")
    rng_count = lax.axis_size("rng")
    group = acq_count * rng_count
    lines, cols = slc.shape[2:]
    tile_lines = 2 * LOOK_A
    halves = BLOCK * tile_lines // lines
    tile_cols = cols // halves
    lanes = 2 * tile_cols // LOOK_R
    wide = 2 * rng_count * cols // LOOK_R
    radar = map_cell.shape[0] * map_cell.shape[1] * rng_count
    piece = MAPC // group
    pairs = acq_count // 2
    dma = pltpu.SemaphoreType.DMA
    result = pl.pallas_call(
        functools.partial(kernel, acq_count, rng_count),
        out_shape=jax.ShapeDtypeStruct((ROUNDS, pairs * 2, piece), F32),
        in_specs=[
            pl.BlockSpec(memory_space=pl.ANY),
            pl.BlockSpec(memory_space=pltpu.VMEM),
        ],
        out_specs=pl.BlockSpec(memory_space=pltpu.VMEM),
        scratch_shapes=[
            pltpu.VMEM((BLOCK, 2, tile_lines, tile_cols), BF16),
            pltpu.VMEM((rng_count,) + map_cell.shape, jnp.int32),
            pltpu.VMEM((group, ROWS, lanes), F32),
            pltpu.VMEM((radar, piece), BF16),
            pltpu.VMEM((tile_cols, lanes), BF16),
            pltpu.VMEM((wide, wide), BF16),
            dma,
            dma((BLOCK,)),
            dma((BLOCK,)),
            dma,
            dma,
            dma((2, group)),
            dma((2, group)),
        ],
        compiler_params=pltpu.CompilerParams(
            collective_id=0, has_side_effects=True, vmem_limit_bytes=40 * 2**20
        ),
    )(slc, map_cell)
    return result.reshape(ROUNDS, pairs, 2, piece)


def solution(mesh):
    in_specs = (P(None, ("groups", "acq"), None, "rng"), P("groups", "rng"))
    out_specs = P(None, "groups", None, ("acq", "rng"))
    return jax.shard_map(
        per_device, mesh=mesh, in_specs=in_specs, out_specs=out_specs, check_vma=False
    )
```

time: 23.7 us -> 23 us (0.970)
  Pallas kernels: 21.1 us -> 20.5 us
    pallas_call x1, Pallas kernels: 21.1 us -> 20.5 us  [per_device(): pl.pallas_call(functools.partial(kernel, acq_count, rng_count), out_shape...]
where the time goes in v2:
time: 23 us; the launch traced here: 22.8 us
  Pallas kernels  20.5 us (89%)
  local copies, waits for them, and re-layouts  2.33 us (10%)
    pallas_call x1, Pallas kernels, per_device(): pl.pallas_call(functools.partial(kernel, acq_count, rng_count), out_shape...  20.5 us
    unnamed x4, local copies, waits for them, and re-layouts  1.64 us
    reshape x1, local copies, waits for them, and re-layouts, per_device(): return result.reshape(ROUNDS, pairs, 2, piece)  0.7 us

profile of v2, /device:TPU:0, one launch (start us, length us, event | category | flops | bytes accessed | tf_op | source)
XLA Modules:
  0.0 22.8 jit_solution(13784967762059486984)
XLA Ops:
  0.0 0.0 copy-start
  0.0 0.9 %copy-done = bf16[2,1,64,1024]{3,2,1,0:T(8,128)(2,1)S(1)} copy-done((bf16[2,1,64,1024]{3,2,1,0:T(8,128)(2,1)S(1)}, bf16[2,1,64,1024]{3,2,1,0:T(8,128)(2,1)}, u32[]{:S(2)}) %copy-start) | copy-done | bytes 262168
  1.0 0.0 copy-start.1
  1.0 0.7 %copy-done.1 = s32[8,128]{1,0:T(8,128)S(1)} copy-done((s32[8,128]{1,0:T(8,128)S(1)}, s32[8,128]{1,0:T(8,128)}, u32[]{:S(2)}) %copy-start.1) | copy-done | bytes 4120
  1.6 20.5 %shard_map.28 = f32[3,8,1024]{2,1,0:T(8,128)S(1)} custom-call(bf16[2,1,64,1024]{3,2,1,0:T(8,128)(2,1)S(1)} %copy-done, s32[8,128]{1,0:T(8,128)S(1)} %copy-done.1), custom_call_target="tpu_custom_call" | custom-call | tf_op jit(solution)/shard_map/pallas_call | solution.py:316
  22.1 0.7 %reshape.3 = f32[3,4,2,1024]{3,2,1,0:T(2,128)} reshape(f32[3,8,1024]{2,1,0:T(8,128)S(1)} %shard_map.28) | data formatting | bytes 196608 | tf_op jit(solution)/shard_map/reshape | solution.py:343
Async XLA Ops:
  0.0 0.9 %copy-start = (bf16[2,1,64,1024]{3,2,1,0:T(8,128)(2,1)S(1)}, bf16[2,1,64,1024]{3,2,1,0:T(8,128)(2,1)}, u32[]{:S(2)}) copy-start(bf16[2,1,64,1024]{3,2,1,0:T(8,128)(2,1)} %slc_ref.1) | copy-start | bytes 786436
  1.0 0.7 %copy-start.1 = (s32[8,128]{1,0:T(8,128)S(1)}, s32[8,128]{1,0:T(8,128)}, u32[]{:S(2)}) copy-start(s32[8,128]{1,0:T(8,128)} %map_ref.1) | copy-start | bytes 12292

commit v3 on v2

--- a/solution.py
+++ b/solution.py
@@ -337,7 +337,7 @@
             dma((2, group)),
         ],
         compiler_params=pltpu.CompilerParams(
-            collective_id=0, has_side_effects=True, vmem_limit_bytes=40 * 2**20
+            collective_id=0, has_side_effects=True, vmem_limit_bytes=int(53.72 * 2**20)
         ),
     )(slc, map_cell)
     return result.reshape(ROUNDS, pairs, 2, piece)

time: 23 us -> 22.3 us (0.970)
  local copies, waits for them, and re-layouts: 2.33 us -> 1.38 us
    unnamed x4 -> x2, local copies, waits for them, and re-layouts: 1.64 us -> 0.69 us
    pallas_call x1, Pallas kernels: 20.5 us -> 20.7 us  [per_device(): pl.pallas_call(functools.partial(kernel, acq_count, rng_count), out_shape...]
where the time goes in v3:
time: 22.3 us; the launch traced here: 22.1 us
  Pallas kernels  20.7 us (93%)
  local copies, waits for them, and re-layouts  1.38 us (6%)
    pallas_call x1, Pallas kernels, per_device(): pl.pallas_call(functools.partial(kernel, acq_count, rng_count), out_shape...  20.7 us
    reshape x1, local copies, waits for them, and re-layouts, per_device(): return result.reshape(ROUNDS, pairs, 2, piece)  0.7 us
    unnamed x2, local copies, waits for them, and re-layouts  0.69 us

profile of v3, /device:TPU:0, one launch (start us, length us, event | category | flops | bytes accessed | tf_op | source)
XLA Modules:
  0.0 22.1 jit_solution(2235684322506508192)
XLA Ops:
  0.0 0.0 copy-start
  0.0 0.7 %copy-done = s32[8,128]{1,0:T(8,128)S(1)} copy-done((s32[8,128]{1,0:T(8,128)S(1)}, s32[8,128]{1,0:T(8,128)}, u32[]{:S(2)}) %copy-start) | copy-done | bytes 4120
  0.7 20.7 %shard_map.28 = f32[3,8,1024]{2,1,0:T(8,128)S(1)} custom-call(bf16[2,1,64,1024]{3,2,1,0:T(8,128)(2,1)} %slc_ref.1, s32[8,128]{1,0:T(8,128)S(1)} %copy-done), custom_call_target="tpu_custom_call" | custom-call | tf_op jit(solution)/shard_map/pallas_call | solution.py:316
  21.4 0.7 %reshape.3 = f32[3,4,2,1024]{3,2,1,0:T(2,128)} reshape(f32[3,8,1024]{2,1,0:T(8,128)S(1)} %shard_map.28) | data formatting | bytes 196608 | tf_op jit(solution)/shard_map/reshape | solution.py:343
Async XLA Ops:
  0.0 0.7 %copy-start = (s32[8,128]{1,0:T(8,128)S(1)}, s32[8,128]{1,0:T(8,128)}, u32[]{:S(2)}) copy-start(s32[8,128]{1,0:T(8,128)} %map_ref.1) | copy-start | bytes 12292

commit v4 on v3

--- a/solution.py
+++ b/solution.py
@@ -87,7 +87,9 @@
             body(0, core)
         if acq_count <= 2 * BLOCK:
             for far in range(1, acq_count):
-                for core in range(rng_count):
+                body(far, 0)
+            for core in range(1, rng_count):
+                for far in range(1, acq_count):
                     body(far, core)
             return
 

time: 22.3 us -> 22.1 us (level)
    pallas_call x1, Pallas kernels: 20.7 us -> 20.5 us  [per_device(): pl.pallas_call(functools.partial(kernel, acq_count, rng_count), out_shape...]
where the time goes in v4:
time: 22.1 us; the launch traced here: 21.9 us
  Pallas kernels  20.5 us (93%)
  local copies, waits for them, and re-layouts  1.38 us (6%)
    pallas_call x1, Pallas kernels, per_device(): pl.pallas_call(functools.partial(kernel, acq_count, rng_count), out_shape...  20.5 us
    reshape x1, local copies, waits for them, and re-layouts, per_device(): return result.reshape(ROUNDS, pairs, 2, piece)  0.7 us
    unnamed x2, local copies, waits for them, and re-layouts  0.69 us

profile of v4, /device:TPU:0, one launch (start us, length us, event | category | flops | bytes accessed | tf_op | source)
XLA Modules:
  0.0 21.9 jit_solution(14992403366380495942)
XLA Ops:
  0.0 0.0 copy-start
  0.0 0.7 %copy-done = s32[8,128]{1,0:T(8,128)S(1)} copy-done((s32[8,128]{1,0:T(8,128)S(1)}, s32[8,128]{1,0:T(8,128)}, u32[]{:S(2)}) %copy-start) | copy-done | bytes 4120
  0.7 20.5 %shard_map.28 = f32[3,8,1024]{2,1,0:T(8,128)S(1)} custom-call(bf16[2,1,64,1024]{3,2,1,0:T(8,128)(2,1)} %slc_ref.1, s32[8,128]{1,0:T(8,128)S(1)} %copy-done), custom_call_target="tpu_custom_call" | custom-call | tf_op jit(solution)/shard_map/pallas_call | solution.py:318
  21.2 0.7 %reshape.3 = f32[3,4,2,1024]{3,2,1,0:T(2,128)} reshape(f32[3,8,1024]{2,1,0:T(8,128)S(1)} %shard_map.28) | data formatting | bytes 196608 | tf_op jit(solution)/shard_map/reshape | solution.py:345
Async XLA Ops:
  0.0 0.7 %copy-start = (s32[8,128]{1,0:T(8,128)S(1)}, s32[8,128]{1,0:T(8,128)}, u32[]{:S(2)}) copy-start(s32[8,128]{1,0:T(8,128)} %map_ref.1) | copy-start | bytes 12292
